TPU v7x, 512 devices: a whole 4x8x8 slice. The times are simulated.
512 devices in a mesh: row: 64 (over y, z), col: 8 (over x, core).
Axes of the slice: x: 4, y: 8, z: 8, core: 2. Of those that a mesh axis runs over, the one named last changes fastest.
Arguments:
- a_tiles: bfloat16 [1024, 7, 4096], P('row'), may hold values from -0.25 to 0.25
- neighbors: int32 [1024, 7], P('row'), may hold values from 0 to 527, as said below
- send_rows: int32 [64, 512], P('row'), may hold values from 0 to 15
- p_tiles: bfloat16 [1024, 8, 4096], P('row', 'col'), may hold values from -0.5 to 0.5
- p_index: int32 [1024, 8], P('row', 'col'), may hold values from 0 to 1
Outputs:
- coarse: float32 [1024, 1024], P('row', 'col')
Inputs may be any that keep to these rules, and one draw needn't show every extreme that they name: `neighbors`: column 0 of a row names the row itself (local index). Other entries below 16 are local rows. An entry v >= 16 names slot s = (v - 16) % 8 filled by device p = (v - 16) // 8, never the reading device itself; s < 8 when p is next to the reader along the row axis (with wrap), s < 4 otherwise.
All inputs are finite; a program needn't handle non-finite values.
Results may differ from a plain program's by a relative error of at most 0.0029.
Values may be sent and summed in bfloat16 or wider, within the bound.
A program may use at most 64 MiB of HBM per device.

v0:
```python
import jax
import jax.numpy as jnp
from jax import lax
from jax.sharding import PartitionSpec as P

B = 64
CP = 2


def widen(tiles, index):
    count = tiles.shape[0]
    blocks = tiles.reshape(count, B, 1, B)
    hit = index[:, None] == jnp.arange(CP)[None, :]
    placed = jnp.where(hit[:, None, :, None], blocks, jnp.zeros((), jnp.bfloat16))
    return placed.reshape(count, B, CP * B)


def shards(a_tiles, neighbors, send_rows, p_tiles, p_index):
    rows = a_tiles.shape[0]
    span = a_tiles.shape[1]
    own_tiles = p_tiles[:, 0, :]
    own_index = p_index[:, 0]
    outgoing = send_rows[0]
    send_tiles = jnp.take(own_tiles, outgoing, axis=0)
    send_index = jnp.take(own_index, outgoing, axis=0)
    ghost_tiles, ghost_index = (
        lax.all_to_all(send_tiles, "row", split_axis=0, concat_axis=0, tiled=True),
        lax.all_to_all(send_index, "row", split_axis=0, concat_axis=0, tiled=True),
    )
    all_tiles = jnp.concatenate([own_tiles, ghost_tiles], axis=0)
    all_index = jnp.concatenate([own_index, ghost_index], axis=0)
    dense_panel = widen(all_tiles, all_index)
    picked = jnp.take(dense_panel, neighbors, axis=0)
    coupling = a_tiles.reshape(rows, span, B, B)
    product = jnp.einsum("rkij,rkjc->ric", coupling, picked, preferred_element_type=jnp.float32)
    product = product.astype(jnp.bfloat16).reshape(rows * B, CP * B)
    panel_tiles, panel_index = (
        lax.all_gather(p_tiles, "col", axis=1, tiled=True),
        lax.all_gather(p_index, "col", axis=1, tiled=True),
    )
    panels = panel_tiles.shape[1]
    blocks = (
        panel_tiles.reshape(rows, panels, B, B).transpose(0, 2, 1, 3).reshape(rows, B, panels, 1, B)
    )
    hit = panel_index[:, :, None] == jnp.arange(CP)[None, None, :]
    wide = jnp.where(hit[:, None, :, :, None], blocks, jnp.zeros((), jnp.bfloat16)).reshape(
        rows * B, panels * CP * B
    )
    return lax.psum_scatter(
        lax.dot_general(
            wide, product, (((0,), (0,)), ((), ())), preferred_element_type=jnp.float32
        ),
        "row",
        scatter_dimension=0,
        tiled=True,
    )


def solution(mesh):
    in_specs = (
        P("row", None, None),
        P("row", None),
        P("row", None),
        P("row", "col", None),
        P("row", "col"),
    )
    out_specs = P("row", "col")
    return jax.shard_map(shards, mesh=mesh, in_specs=in_specs, out_specs=out_specs, check_vma=False)
```

profile of v0, /device:TPU:1, one launch (start us, length us, event | category | flops | bytes accessed | tf_op | source)
XLA Modules:
  0.0 436.3 jit_solution(14286132359882156465)
XLA Ops:
  6.5 1.9 fusion.16
  8.5 0.7 compare_select_fusion.2
  9.2 9.9 %select_select_fusion = s32[512]{0:T(512)S(1)} fusion(s32[512]{0:T(512)S(1)} %bitcast.66, s32[]{:T(128)} %bitcast.7, s32[]{:T(128)} %bitcast.8, s32[]{:T(128)} %bitcast.9, s32[]{:T(128)} %bitcast.10, s32[]{:T(128)} %bitcast.11, s32[]{:T(128)} %bitcast.12, s32[]{:T(128)} %bitcast.13, s32[]{:T(128)} %bitcast.14, s32[]{:T(128)} %bitcast.15, s32[]{:T(128)} %bitcast.16, ...), kind=kLoop, calls=%fused_computation.25 | loop fusion | flops 15360 | bytes 4160 | tf_op jit(solution)/shard_map/jit(_take)/gather | solution.py:25
  19.1 0.1 gather.17
  19.2 0.5 broadcast.189
  19.7 1.3 reduce.8
  21.1 0.1 squeeze.14
  21.2 0.6 and_select_fusion
  21.8 17.1 %all-to-all-start = ((s32[64,8,1]{1,2,0:T(1,128)}), s32[64,8,1]{1,2,0:T(1,128)S(1)}, u32[]{:S(2)}, u32[]{:S(2)}) async-start(s32[64,8,1]{1,2,0:T(1,128)} %bitcast.23), calls=%async_computation | async-start | bytes 65536 | tf_op jit(solution)/shard_map/all_to_all | solution.py:28
  38.9 0.8 squeeze.16
  39.7 4.4 %gather_fusion = bf16[512,4096]{1,0:T(8,128)(2,1)} fusion(bf16[16,4096]{1,0:T(8,128)(2,1)S(1)} %bitcast.57, s32[1024]{0:T(1024)S(1)} %pad_clamp_fusion.1), kind=kCustom, calls=%fused_computation | custom fusion | bytes 8390656 | tf_op jit(solution)/shard_map/jit(_take)/gather | solution.py:24
  44.2 4.6 %bitcast_select_fusion = bf16[64,8,4096]{2,1,0:T(8,128)(2,1)} fusion(bf16[512,4096]{1,0:T(8,128)(2,1)} %gather_fusion, pred[64,8]{1,0:T(8,128)(4,1)S(1)} %compare_and_fusion), kind=kLoop, calls=%fused_computation.4 | loop fusion | flops 2097152 | bytes 8389120 | tf_op jit(solution)/shard_map/jit(_take)/select_n | solution.py:24
  48.7 1.0 all-to-all-done
  49.8 11.5 %all-to-all-start.1 = ((bf16[64,8,4096]{2,1,0:T(8,128)(2,1)}), bf16[64,8,4096]{2,1,0:T(8,128)(2,1)}, u32[]{:S(2)}, u32[]{:S(2)}) async-start(bf16[64,8,4096]{2,1,0:T(8,128)(2,1)} %bitcast_select_fusion), calls=%async_computation.1 | async-start | bytes 8388608 | tf_op jit(solution)/shard_map/all_to_all | solution.py:27
  61.3 0.0 all-gather.3.cloned.1.call-start
  61.4 0.7 all-gather.3.cloned.1.call-update
  62.0 0.0 all-reduce.3.cloned.1.call-start
  62.1 0.2 concatenate.12
  62.4 0.1 copy.52
  62.5 0.1 reshape.188
  62.6 3.0 reshape.153
  65.5 0.1 copy.47
  65.6 12.0 %all-gather = s32[8,1,16]{2,1,0:T(1,128)S(1)} all-gather(s32[1,1,16]{2,1,0:T(1,128)S(1)} %bitcast.63), channel_id=1, replica_groups=mesh['row'=64,'col'=8] {'col'}, dimensions={0}, use_global_device_ids=true | all-gather | bytes 576 | tf_op jit(solution)/shard_map/all_gather | solution.py:39
  77.6 0.1 copy.44
  77.7 0.7 reduce.9
  78.4 0.1 all_to_all.11
  78.5 0.1 pad_add_fusion
  78.6 0.2 copy.49
  78.8 16.1 %all-gather.3.cloned.1.call-done = bf16[16,8,4096]{2,0,1:T(8,128)(2,1)} async-done(((bf16[16,1,4096]{2,0,1:T(8,128)(2,1)}), bf16[16,8,4096]{2,0,1:T(8,128)(2,1)}) %all-gather.3.cloned.1.call-update) | async-done | bytes 1048592 | tf_op jit(solution)/shard_map/all_gather | solution.py:38
  95.0 3.3 reshape.152
  98.2 1.8 copy.45
  100.0 2.4 broadcast_select_fusion.1
  102.4 6.6 %copy.46 = bf16[16,64,8,2,64]{1,0,4,3,2:T(8,128)(2,1)} copy(bf16[16,64,8,2,64]{4,2,3,1,0:T(8,128)(2,1)} %broadcast_select_fusion.1) | data formatting | bytes 4194304 | tf_op jit(solution)/shard_map/jit(_where)/select_n | solution.py:46
  109.0 5.5 %select_n.73 = bf16[1024,1024]{0,1:T(8,128)(2,1)S(1)} reshape(bf16[16,64,8,2,64]{1,0,4,3,2:T(8,128)(2,1)} %copy.46) | data formatting | bytes 4194304 | tf_op jit(solution)/shard_map/jit(_where)/select_n | solution.py:46
  114.5 67.4 %all-to-all-done.1 = bf16[64,8,4096]{2,1,0:T(8,128)(2,1)} async-done(((bf16[64,8,4096]{2,1,0:T(8,128)(2,1)}), bf16[64,8,4096]{2,1,0:T(8,128)(2,1)}, u32[]{:S(2)}, u32[]{:S(2)}) %all-to-all-start.1) | async-done | bytes 4194336 | tf_op jit(solution)/shard_map/all_to_all | solution.py:27
  181.9 12.5 %concatenate.13 = bf16[512,64,1,64]{3,1,0,2:T(8,128)(2,1)} reshape(bf16[64,8,4096]{2,1,0:T(8,128)(2,1)} %all-to-all-done.1) | data formatting | bytes 8388608 | tf_op jit(solution)/shard_map/concatenate | solution.py:30
  194.5 8.4 %maximum_bitcast_fusion = bf16[528,64,64]{2,1,0:T(8,128)(2,1)} fusion(bf16[512,64,1,64]{3,1,0,2:T(8,128)(2,1)} %concatenate.13, bf16[16,64,1,64]{3,1,0,2:T(8,128)(2,1)S(1)} %concatenate.12), kind=kLoop, calls=%fused_computation.2 | loop fusion | flops 2162688 | bytes 8650752 | tf_op jit(solution)/shard_map/jit(_where)/broadcast_in_dim | solution.py:14
  202.9 13.6 %copy.50 = bf16[528,64,64]{0,2,1:T(8,128)(2,1)} copy(bf16[528,64,64]{2,1,0:T(8,128)(2,1)} %maximum_bitcast_fusion) | data formatting | bytes 8650752 | tf_op jit(solution)/shard_map/jit(_where)/broadcast_in_dim | solution.py:14
  216.5 8.1 %broadcast_in_dim.93 = bf16[528,64,2,64]{0,3,2,1:T(8,128)(2,1)} broadcast(bf16[528,64,64]{0,2,1:T(8,128)(2,1)} %copy.50), dimensions={0,1,3} | broadcast | bytes 12976128 | tf_op jit(solution)/shard_map/jit(_where)/broadcast_in_dim | solution.py:14
  224.5 14.4 %copy.51 = bf16[528,64,128]{2,1,0:T(8,128)(2,1)} copy(bf16[528,64,128]{0,2,1:T(8,128)(2,1)} %bitcast.58) | data formatting | bytes 17301504 | tf_op jit(solution)/shard_map/jit(_where)/broadcast_in_dim | solution.py:14
  238.9 7.6 %broadcast_select_fusion = bf16[528,64,128]{2,1,0:T(8,128)(2,1)} fusion(bf16[528,64,128]{2,1,0:T(8,128)(2,1)} %copy.51, pred[528,128]{1,0:T(8,128)(4,1)S(1)} %copy.49), kind=kLoop, calls=%fused_computation.3 | loop fusion | flops 4325376 | bytes 17369088 | tf_op jit(solution)/shard_map/jit(_where)/select_n | solution.py:14
  246.6 5.5 %gather_fusion.1 = bf16[112,64,128]{2,1,0:T(8,128)(2,1)} fusion(bf16[528,64,128]{2,1,0:T(8,128)(2,1)} %broadcast_select_fusion, s32[1024]{0:T(1024)S(1)} %pad_clamp_fusion), kind=kCustom, calls=%fused_computation.1 | custom fusion | bytes 3670464 | tf_op jit(solution)/shard_map/jit(_take)/gather | solution.py:33
  252.1 2.8 fusion.9
  254.9 1.5 fusion.17
  256.4 0.0 all-reduce.3.cloned.1.call-update
  256.4 1.3 dynamic-slice
  258.4 169.8 %all-reduce.3.cloned.1.call-done = f32[1024,128]{1,0:T(8,128)} async-done(((f32[1024,128]{1,0:T(8,128)}), f32[1024,128]{1,0:T(8,128)}) %all-reduce.3.cloned.1.call-update) | async-done | bytes 524304
  428.1 1.3 constant_dynamic-slice_fusion
  (18 shorter events, 0.1 us)
Async XLA Ops:
  6.5 33.2 %copy-start = (bf16[16,1,4096]{2,0,1:T(8,128)(2,1)S(1)}, bf16[16,1,4096]{2,0,1:T(8,128)(2,1)}, u32[]{:S(2)}) copy-start(bf16[16,1,4096]{2,0,1:T(8,128)(2,1)} %param.8) | copy-start | bytes 393220
  21.8 28.0 %all-to-all-start = ((s32[64,8,1]{1,2,0:T(1,128)}), s32[64,8,1]{1,2,0:T(1,128)S(1)}, u32[]{:S(2)}, u32[]{:S(2)}) async-start(s32[64,8,1]{1,2,0:T(1,128)} %bitcast.23), calls=%async_computation | async-start | bytes 65536 | tf_op jit(solution)/shard_map/all_to_all | solution.py:28
  48.7 13.4 %copy-start.1 = (bf16[16,1,4096]{2,0,1:T(8,128)(2,1)S(1)}, bf16[16,1,4096]{2,0,1:T(8,128)(2,1)}, u32[]{:S(2)}) copy-start(bf16[16,1,4096]{2,0,1:T(8,128)(2,1)} %param.8) | copy-start | bytes 393220
  48.7 13.6 %copy-start.4 = (s32[16,7]{0,1:T(8,128)S(1)}, s32[16,7]{0,1:T(8,128)}, u32[]{:S(2)}) copy-start(s32[16,7]{0,1:T(8,128)} %param.6) | copy-start | bytes 1348
  48.7 13.8 %copy-start.2 = (bf16[16,7,4096]{2,0,1:T(8,128)(2,1)S(1)}, bf16[16,7,4096]{2,0,1:T(8,128)(2,1)}, u32[]{:S(2)}) copy-start(bf16[16,7,4096]{2,0,1:T(8,128)(2,1)} %param.5) | copy-start | bytes 2752516
  48.7 16.9 %copy-start.3 = (s32[16,1]{0,1:T(1,128)S(1)}, s32[16,1]{0,1:T(1,128)}, u32[]{:S(2)}) copy-start(s32[16,1]{0,1:T(1,128)} %param.9) | copy-start | bytes 196
  49.8 132.2 %all-to-all-start.1 = ((bf16[64,8,4096]{2,1,0:T(8,128)(2,1)}), bf16[64,8,4096]{2,1,0:T(8,128)(2,1)}, u32[]{:S(2)}, u32[]{:S(2)}) async-start(bf16[64,8,4096]{2,1,0:T(8,128)(2,1)} %bitcast_select_fusion), calls=%async_computation.1 | async-start | bytes 8388608 | tf_op jit(solution)/shard_map/all_to_all | solution.py:27
  61.3 33.7 %all-gather.3.cloned.1.call-start = ((), (), s32[]{:S(2)}) async-start(), calls=%async_computation.2 | async-start | bytes 1179648 | tf_op jit(solution)/shard_map/all_gather | solution.py:38
  62.0 366.1 %all-reduce.3.cloned.1.call-start = ((), (), s32[]{:S(2)}) async-start(), calls=%async_computation.3 | async-start | bytes 1048576
Sparse Core Ops, SparseCore 0:
  64.3 30.6 all-gather.2
  256.6 171.5 all-reduce.2
where the time goes:
time: 441 us; the launch traced here: 436 us
  waiting for transfers between devices  255 us (58%)
  local copies, waits for them, and re-layouts  85.4 us (19%)
  other arithmetic  36.5 us (8%)
  starting transfers between devices  28.8 us (7%)
  between operations  14.2 us (3%)
  blocking collectives  12 us (3%)
    unnamed x3, waiting for transfers between devices  170 us
    all_to_all x1, waiting for transfers between devices, shards(): lax.all_to_all(send_tiles, 'row', split_axis=0, concat_axis=0, tiled=True)  67.4 us
    broadcast_in_dim x5, local copies, waits for them, and re-layouts, widen(): jnp.where(hit[:, None, :, None], blocks, jnp.zeros((), jnp.bfloat16))  36.3 us
    all_to_all x1, starting transfers between devices, shards(): lax.all_to_all(send_index, 'row', split_axis=0, concat_axis=0, tiled=True)  17.1 us
    all_gather x1, waiting for transfers between devices, shards(): lax.all_gather(p_tiles, 'col', axis=1, tiled=True)  16.1 us
    concatenate x2, local copies, waits for them, and re-layouts, shards(): all_tiles = jnp.concatenate([own_tiles, ghost_tiles], axis=0)  12.8 us
    select_n x2, local copies, waits for them, and re-layouts, shards(): jnp.where(hit[:, None, :, :, None], blocks, jnp.zeros((), jnp.bfloat16))  12.1 us
    all_gather x1, blocking collectives, shards(): lax.all_gather(p_index, 'col', axis=1, tiled=True)  12 us
  transfers between devices with their start and end apart: 4, of which 4 were waited for; matrix products, arithmetic and copies ran while one was open for 8% of the time, Pallas kernels for 0%

commit v1 on v0

v1 whole, which is shorter than its diff:
```python
import functools

import jax
import jax.numpy as jnp
from jax import lax
from jax.experimental import pallas as pl
from jax.experimental.pallas import tpu as pltpu
from jax.sharding import PartitionSpec as P

MESH = pl.DeviceIdType.MESH
LINE = 8
R = 16
K = 7
GROUPS = R * K // 8
F32, BF16, I32 = jnp.float32, jnp.bfloat16, jnp.int32
META1, SPREAD_Y, SPREAD_Z, PANEL, PINDEX, META2, FWD_Y, FWD_Z, REQ_Y, REQ_Z, GHOST_Y, GHOST_Z, SUM_Y, SUM_Z, LAST_Y, LAST_Z = range(16)


def iota(shape, dim):
    return lax.broadcasted_iota(I32, shape, dim)


def kernel(
    p_ref, p2_ref, a_ref, meta_ref, want_ref, idx_ref, out_ref,
    store_y, store_z, meta_y, meta_all, table, request, req_y, req_z,
    pack_y, pack_z, ghost, panel, idx_all, pick, spread, terms, lhs, wide,
    ap, apb, partial, send_y, send_z, sum_y, sum_z, half_y, half_z, last_y, last_z,
    send_sem, recv_sem,
):
    row, c = lax.axis_index("row"), lax.axis_index("col")
    y, z = row // LINE, row % LINE
    place = {"y": y, "z": z, "c": c}

    def target(axis, t):
        if axis == "y":
            return (t * LINE + z, c)
        if axis == "z":
            return (y * LINE + t, c)
        return (row, t)

    def others(axis):
        return [(place[axis] + d) % LINE for d in range(1, LINE)]

    def copy(phase, axis, t, src, dst, mine):
        return pltpu.make_async_remote_copy(
            src_ref=src, dst_ref=dst, send_sem=send_sem.at[phase, t], recv_sem=recv_sem.at[phase, mine],
            device_id=target(axis, t), device_id_type=MESH,
        )

    started = []

    def push(phase, axis, src, dst):
        me = place[axis]
        for t in others(axis):
            op = copy(phase, axis, t, src(t), dst(me), me)
            op.start()
            started.append(op)

    def arrived(phase, axis, dst):
        for t in others(axis):
            copy(phase, axis, t, dst(t), dst(t), t).wait_recv()

    barrier = pltpu.get_barrier_semaphore()
    for axis in ("y", "z", "c"):
        for t in others(axis):
            pl.semaphore_signal(barrier, inc=1, device_id=target(axis, t), device_id_type=MESH)
    pl.semaphore_wait(barrier, 3 * (LINE - 1))

    def stripe(s):
        return pl.ds(pl.multiple_of(s * 256, 256), 256)

    def rows(start, count):
        return pl.ds(pl.multiple_of(start, count), count)

    push(META1, "y", lambda t: meta_ref.at[t], lambda s: meta_y.at[s])
    push(SPREAD_Y, "y", lambda t: p_ref.at[:, stripe(t)], lambda s: store_y.at[rows(z * 128 + s * R, R)])
    push(SPREAD_Z, "z", lambda t: p_ref.at[:, stripe(LINE + t)], lambda s: store_z.at[rows(y * 128 + s * R, R)])
    meta_y[y] = meta_ref[y]
    store_y[rows(z * 128 + y * R, R)] = p_ref[:, stripe(y)]
    store_z[rows(y * 128 + z * R, R)] = p_ref[:, stripe(LINE + z)]
    arrived(META1, "y", lambda s: meta_y.at[s])
    push(META2, "z", lambda t: meta_y, lambda s: meta_all.at[s])
    arrived(SPREAD_Y, "y", lambda s: store_y.at[rows(z * 128 + s * R, R)])
    push(FWD_Y, "z", lambda t: store_y.at[rows(z * 128, 128)], lambda s: store_y.at[rows(s * 128, 128)])
    arrived(SPREAD_Z, "z", lambda s: store_z.at[rows(y * 128 + s * R, R)])
    push(FWD_Z, "y", lambda t: store_z.at[rows(y * 128, 128)], lambda s: store_z.at[rows(s * 128, 128)])

    panel[c] = p2_ref[...].astype(F32).T.astype(BF16)
    idx_all[c] = idx_ref[...]
    push(PANEL, "c", lambda t: panel.at[c], lambda s: panel.at[s])
    push(PINDEX, "c", lambda t: idx_all.at[c], lambda s: idx_all.at[s])

    meta_all[z] = meta_y[...]
    arrived(META2, "z", lambda s: meta_all.at[s])
    for s in range(LINE):
        for t in range(LINE):
            table[pl.ds(t * LINE + s, 1), :] = meta_all[s, t]
    rows_of = table[...].astype(F32)
    source = iota((64, 128), 0)
    lane = iota((64, 128), 1)
    want = want_ref[...]
    remote = want - R
    total = jnp.zeros((64, 128), F32)
    for s in range(LINE):
        column = jnp.sum(jnp.where(lane == z * LINE + s, rows_of, 0.0), axis=1, keepdims=True)
        value = column + (source * R).astype(F32)
        total = total + jnp.where(source * LINE + s == remote, value, 0.0)
    fine = jnp.where(want < R, want + row * R, jnp.sum(total, axis=0, keepdims=True).astype(I32))
    request[...] = fine
    req_y[y] = fine
    req_z[z] = fine
    push(REQ_Y, "y", lambda t: request, lambda s: req_y.at[s])
    push(REQ_Z, "z", lambda t: request, lambda s: req_z.at[s])
    total = jnp.zeros((64, 128), F32)
    for t in range(R):
        total = total + jnp.where(source * R + t == fine, rows_of[:, 64 + t : 65 + t], 0.0)
    half_of = jnp.sum(total, axis=0, keepdims=True)

    def make_pick(n, _):
        r = iota((128, 1), 0)
        col = (r & 63)
        f = ((r >> 6) & 1) * 512 + (col & 1) * 256 + (col >> 2) * 16 + ((col >> 1) & 1) * 8 + n
        pick[rows(n * 128, 128), :] = jnp.where(iota((128, 1024), 1) == f, 1.0, 0.0).astype(BF16)
        return 0

    lax.fori_loop(0, 8, make_pick, 0)

    def make_spread(b, _):
        first = 8 * b // K
        for slot in range(8):
            j = 8 * b + slot
            i = j // K
            block = a_ref[(j % K) * R + i].astype(F32)
            low = jnp.where(i == first, 1.0, 0.0)
            spread[rows(b * 64, 32), slot * 128 : slot * 128 + 128] = (block * low).astype(BF16)
            spread[rows(b * 64 + 32, 32), slot * 128 : slot * 128 + 128] = (block * (1.0 - low)).astype(BF16)
        return 0

    lax.fori_loop(0, GROUPS, make_spread, 0)
    for n in range(4):
        terms[n] = jnp.dot(
            spread[...], pick[:, n * 256 : n * 256 + 256], preferred_element_type=F32
        ).astype(BF16)

    eye = iota((128, 128), 0) == iota((128, 128), 1)

    def serve(req, t, store, pack, swap):
        asked = req[t]
        column = jnp.sum(jnp.where(eye, asked, 0).astype(F32), axis=1, keepdims=True)[: GROUPS * 8].astype(I32)
        n = iota((1, 1024), 1)
        if swap:
            n = ((n >> 4) & 7) * 128 + (n >> 7) * R + (n & 15)
        hot = jnp.where(n == column, 1.0, 0.0).astype(BF16)
        got = jnp.dot(hot, store[...], preferred_element_type=F32)
        got = got.reshape(GROUPS, 8, 256)
        return jnp.concatenate([got[:, :, :128], got[:, :, 128:]], axis=1).astype(BF16)

    arrived(REQ_Y, "y", lambda s: req_y.at[s])
    arrived(FWD_Y, "z", lambda s: store_y.at[rows(s * 128, 128)])
    for t in others("y"):
        pack_y[t] = serve(req_y, t, store_y, pack_y, True)
        op = copy(GHOST_Y, "y", t, pack_y.at[t], ghost.at[:, rows(y * 16, 16), :], y)
        op.start()
        started.append(op)
    arrived(REQ_Z, "z", lambda s: req_z.at[s])
    arrived(FWD_Z, "y", lambda s: store_z.at[rows(s * 128, 128)])
    for t in others("z"):
        pack_z[t] = serve(req_z, t, store_z, pack_z, False)
        op = copy(GHOST_Z, "z", t, pack_z.at[t], ghost.at[:, rows(128 + z * 16, 16), :], z)
        op.start()
        started.append(op)
    ghost[:, rows(y * 16, 16), :] = serve(req_y, y, store_y, pack_y, True)
    ghost[:, rows(128 + z * 16, 16), :] = serve(req_z, z, store_z, pack_z, False)

    by_group = jnp.where(iota((GROUPS + 2, 128), 1) >> 3 == iota((GROUPS + 2, 128), 0), half_of, 0.0)
    by_slot = jnp.where((iota((128, 256), 0) & 7) == (iota((128, 256), 1) & 7), 1.0, 0.0)
    mask = jnp.dot(by_group.astype(BF16), by_slot.astype(BF16), preferred_element_type=F32)
    for b in range(GROUPS):
        upper = mask[b : b + 1]
        for h, m in ((0, 1.0 - upper), (1, upper)):
            for n in range(4):
                lhs[b, h * 256 + n * 64 : h * 256 + n * 64 + 64, :] = (
                    terms[n, b * 64 : b * 64 + 64, :] * m.astype(BF16)
                )
    arrived(PANEL, "c", lambda s: panel.at[s])
    arrived(PINDEX, "c", lambda s: idx_all.at[s])

    def make_wide(n, _):
        upper = idx_all[n].astype(F32)
        for h, m in ((0, 1.0 - upper), (1, upper)):
            for pr in range(2):
                wide[rows(n * 128 + h * 64, 64), pr * 512 : pr * 512 + 512] = (
                    panel[n, pr * 64 : pr * 64 + 64, :] * m.astype(BF16)
                )
        return 0

    lax.fori_loop(0, LINE, make_wide, 0)
    ap[...] = jnp.zeros_like(ap)

    arrived(GHOST_Y, "y", lambda s: ghost.at[:, rows(s * 16, 16), :])
    arrived(GHOST_Z, "z", lambda s: ghost.at[:, rows(128 + s * 16, 16), :])

    left = iota((64, 128), 1) < 64

    def multiply(b, _):
        out = jnp.dot(lhs[b], ghost[b], preferred_element_type=F32)
        start = pl.multiple_of((8 * b // K) * 32, 32)
        for pr in range(2):
            u0 = out[pr * 128 : pr * 128 + 64]
            u1 = out[pr * 128 + 64 : pr * 128 + 128]
            v0 = out[256 + pr * 128 : 256 + pr * 128 + 64]
            v1 = out[256 + pr * 128 + 64 : 256 + pr * 128 + 128]
            ap[pr, pl.ds(start, 64), :] += jnp.where(left, u0 + pltpu.roll(u1, 64, 1), pltpu.roll(v0, 64, 1) + v1)
        return 0

    lax.fori_loop(0, GROUPS, multiply, 0)
    for pr in range(2):
        apb[pr * 512 : pr * 512 + 512] = ap[pr].astype(BF16)

    def project(n, _):
        block = jnp.dot(wide[rows(n * 128, 128), :], apb[...], preferred_element_type=F32)
        partial[n] = block.reshape(LINE, 2, 8, 128)
        return 0

    lax.fori_loop(0, LINE, project, 0)
    for n in range(LINE):
        send_y[n] = partial[n, :, 0].reshape(64, 128).astype(BF16)
    push(SUM_Y, "y", lambda t: send_y.at[t], lambda s: sum_y.at[s])
    for n in range(LINE):
        send_z[n] = partial[:, n, 1].reshape(64, 128).astype(BF16)
    push(SUM_Z, "z", lambda t: send_z.at[t], lambda s: sum_z.at[s])
    arrived(SUM_Y, "y", lambda s: sum_y.at[s])
    acc = partial[y, :, 0].reshape(64, 128)
    for t in others("y"):
        acc = acc + sum_y[t].astype(F32)
    half_y[...] = acc.reshape(LINE, 8, 128)
    push(LAST_Y, "z", lambda t: half_y.at[t], lambda s: last_y.at[s])
    arrived(SUM_Z, "z", lambda s: sum_z.at[s])
    acc = partial[:, z, 1].reshape(64, 128)
    for t in others("z"):
        acc = acc + sum_z[t].astype(F32)
    half_z[...] = acc.reshape(LINE, 8, 128)
    push(LAST_Z, "y", lambda t: half_z.at[t], lambda s: last_z.at[s])
    arrived(LAST_Y, "z", lambda s: last_y.at[s])
    acc = half_y[z]
    for t in others("z"):
        acc = acc + last_y[t]
    out_ref[0:8] = acc
    arrived(LAST_Z, "y", lambda s: last_z.at[s])
    acc = half_z[y]
    for t in others("y"):
        acc = acc + last_z[t]
    out_ref[8:16] = acc
    for op in started:
        op.wait_send()


def shards(a_tiles, neighbors, send_rows, p_tiles, p_index):
    tiles = p_tiles.reshape(R, 4096)
    tall = tiles.reshape(R * 32, 128)
    blocks = a_tiles.transpose(1, 0, 2).reshape(K * R, 32, 128)
    meta = jnp.concatenate(
        [
            send_rows.reshape(LINE, 1, 64),
            jnp.broadcast_to(p_index.reshape(1, 1, R), (LINE, 1, R)),
            jnp.zeros((LINE, 1, 128 - 64 - R), I32),
        ],
        axis=2,
    )
    want = jnp.pad(neighbors.reshape(1, R * K), ((0, 0), (0, 128 - R * K)))
    index = jnp.repeat(p_index.reshape(1, R), 32, axis=1)
    vmem = pl.BlockSpec(memory_space=pltpu.VMEM)
    V = pltpu.VMEM
    return pl.pallas_call(
        kernel,
        out_shape=jax.ShapeDtypeStruct((R, 128), F32),
        in_specs=[vmem] * 6,
        out_specs=vmem,
        scratch_shapes=[
            V((1024, 256), BF16), V((1024, 256), BF16),
            V((LINE, 1, 128), I32), V((LINE, LINE, 1, 128), I32), V((64, 128), I32),
            V((1, 128), I32), V((LINE, 1, 128), I32), V((LINE, 1, 128), I32),
            V((LINE, GROUPS, 16, 128), BF16), V((LINE, GROUPS, 16, 128), BF16),
            V((GROUPS, 256, 128), BF16),
            V((LINE, 128, 512), BF16), V((LINE, 1, 512), I32),
            V((1024, 1024), BF16), V((GROUPS * 64, 1024), BF16), V((4, GROUPS * 64, 256), BF16),
            V((GROUPS, 512, 256), BF16), V((1024, 1024), BF16),
            V((2, 512, 128), F32), V((1024, 128), BF16), V((LINE, LINE, 2, 8, 128), F32),
            V((LINE, 64, 128), BF16), V((LINE, 64, 128), BF16),
            V((LINE, 64, 128), BF16), V((LINE, 64, 128), BF16),
            V((LINE, 8, 128), F32), V((LINE, 8, 128), F32),
            V((LINE, 8, 128), F32), V((LINE, 8, 128), F32),
            pltpu.SemaphoreType.DMA((16, LINE)), pltpu.SemaphoreType.DMA((16, LINE)),
        ],
        compiler_params=pltpu.CompilerParams(
            collective_id=0, has_side_effects=True, vmem_limit_bytes=48 * 2**20
        ),
    )(tiles, tall, blocks, meta, want, index)


def solution(mesh):
    in_specs = (
        P("row", None, None),
        P("row", None),
        P("row", None),
        P("row", "col", None),
        P("row", "col"),
    )
    return jax.shard_map(shards, mesh=mesh, in_specs=in_specs, out_specs=P("row", "col"), check_vma=False)
```

time: 441 us -> 72.7 us (0.16)
  waiting for transfers between devices: 255 us -> 0 us
  local copies, waits for them, and re-layouts: 85.4 us -> 5.48 us
  Pallas kernels: 0 us -> 65.3 us
  other arithmetic: 36.5 us -> 0.67 us
  starting transfers between devices: 28.8 us -> 0 us
  between operations: 14.2 us -> 0.06 us
  blocking collectives: 12 us -> 0 us
    unnamed x3 -> x0, waiting for transfers between devices: 170 us -> none
    all_to_all x2 -> x0, waiting for transfers between devices: 68.5 us -> none  [the longest x1 67.4 us: shards(): lax.all_to_all(send_tiles, 'row', split_axis=0, concat_axis=0, tiled=True)]
    pallas_call x0 -> x1, Pallas kernels: none -> 65.3 us  [shards(): pl.pallas_call(kernel, out_shape=jax.ShapeDtypeStruct((R, 128), F32), in_...]
    broadcast_in_dim x6 -> x3, local copies, waits for them, and re-layouts: 36.4 us -> 0.15 us  [the longest x2 0.15 us: shards(): index = jnp.repeat(p_index.reshape(1, R), 32, axis=1)]
    all_to_all x2 -> x0, starting transfers between devices: 28.7 us -> none  [the longest x1 17.1 us: shards(): lax.all_to_all(send_index, 'row', split_axis=0, concat_axis=0, tiled=True)]
    all_gather x1 -> x0, waiting for transfers between devices: 16.1 us -> none  [shards(): lax.all_gather(p_tiles, 'col', axis=1, tiled=True)]
    select_n x6 -> x0, other arithmetic: 15.9 us -> none  [the longest x1 7.64 us: widen(): jnp.where(hit[:, None, :, None], blocks, jnp.zeros((), jnp.bfloat16))]
    concatenate x2, local copies, waits for them, and re-layouts: 12.8 us -> 0.15 us  [shards(): jnp.concatenate([send_rows.reshape(LINE, 1, 64), jnp.broadcast_to(p_index...]
  transfers between devices with their start and end apart: 4 -> 0, of which waited for: 4 -> 0; matrix products, arithmetic and copies ran while one was open for 8% -> 0% of each run, Pallas kernels for 0% -> 0%
where the time goes in v1:
time: 72.7 us; the launch traced here: 71.6 us
  Pallas kernels  65.3 us (90%)
  local copies, waits for them, and re-layouts  5.48 us (8%)
    pallas_call x1, Pallas kernels, shards(): pl.pallas_call(kernel, out_shape=jax.ShapeDtypeStruct((R, 128), F32), in_...  65.3 us
    unnamed x12, local copies, waits for them, and re-layouts  4.03 us

profile of v1, /device:TPU:1, one launch (start us, length us, event | category | flops | bytes accessed | tf_op | source)
XLA Modules:
  0.0 71.6 jit_solution(7892420450314084371)
XLA Ops:
  0.0 0.0 copy-start.3
  0.0 0.7 copy-done.3
  0.7 0.1 pad.6.clone
  0.7 0.0 copy-start.2
  0.7 0.1 pad.7.clone
  0.8 0.5 broadcast.13
  1.3 0.1 copy-done.2
  1.4 0.7 reduce.3
  2.1 0.1 reshape.25
  2.2 0.0 copy-start.1
  2.2 0.7 copy-done.1
  2.9 0.1 copy.7
  2.9 0.1 reshape.26
  3.0 0.1 broadcast_in_dim.18
  3.1 0.1 broadcast_in_dim.19.idx_ref
  3.2 1.0 %reshape_reshape.3.p2_ref = bf16[512,128]{1,0:T(8,128)(2,1)S(1)} reshape(bf16[16,1,4096]{2,0,1:T(8,128)(2,1)} %param.8) | data formatting | bytes 262144 | tf_op jit(solution)/shard_map/reshape;reshape | solution.py:260
  4.2 0.0 copy-start
  4.2 1.4 %copy.8 = bf16[14,8,32,128]{3,2,1,0:T(8,128)(2,1)S(1)} copy(bf16[14,8,32,128]{3,1,2,0:T(8,128)(2,1)} %bitcast.10) | data formatting | bytes 1835008
  5.6 0.0 copy-done
  5.6 65.3 %shard_map.55 = f32[16,128]{1,0:T(8,128)S(1)} custom-call(bf16[16,4096]{1,0:T(8,128)(2,1)S(1)} %bitcast.9, bf16[512,128]{1,0:T(8,128)(2,1)S(1)} %reshape_reshape.3.p2_ref, bf16[112,32,128]{2,1,0:T(8,128)(2,1)S(1)} %bitcast.8, s32[8,1,128]{2,1,0:T(1,128)S(1)} %add_add_fusion.meta_ref, s32[1,128]{1,0:T(1,128)S(1)} %pad.4.want_ref, ...), custom_call_target="tpu_custom_call" | custom-call | tf_op jit(solution)/shard_map/pallas_call | solution.py:274
  70.9 0.6 copy.10
  (3 shorter events, 0.0 us)
Async XLA Ops:
  0.0 0.7 copy-start.3
  0.7 0.7 copy-start.2
  2.2 0.7 copy-start.1
  4.2 1.4 %copy-start = (bf16[16,1,4096]{2,0,1:T(8,128)(2,1)S(1)}, bf16[16,1,4096]{2,0,1:T(8,128)(2,1)}, u32[]{:S(2)}) copy-start(bf16[16,1,4096]{2,0,1:T(8,128)(2,1)} %param.8) | copy-start | bytes 393220

commit v2 on v1

v2 whole, which is shorter than its diff:
```python
import functools

import jax
import jax.numpy as jnp
from jax import lax
from jax.experimental import pallas as pl
from jax.experimental.pallas import tpu as pltpu
from jax.sharding import PartitionSpec as P

MESH = pl.DeviceIdType.MESH
LINE = 8
R = 16
K = 7
FAR = K - 1
ASKED = R * FAR
GROUPS = ASKED // 8
F32, BF16, I32 = jnp.float32, jnp.bfloat16, jnp.int32
META1, SPREAD_Y, SPREAD_Z, PANEL, PINDEX, META2, FWD_Y, FWD_Z, REQ_Y, REQ_Z, GHOST_Y, GHOST_Z, SUM_Y, SUM_Z, LAST_Y, LAST_Z, NEXT_Y, NEXT_Z = range(18)


def iota(shape, dim):
    return lax.broadcasted_iota(I32, shape, dim)


def kernel(
    p_ref, a_ref, near_ref, sends_ref, index_ref, out_ref,
    raw, meta, store_y, store_z, meta_y, meta_all, table, request, req_y, req_z, hot_y, hot_z,
    pack_y, pack_z, ghost, panel, idx_all, order, tall, natural, own, pick, spread, terms, lhs, wide,
    own_pick, own_spread, own_terms,
    ap, apb, partial, send_y, send_z, sum_y, sum_z, half_y, half_z, last_y, last_z,
    send_sem, recv_sem, local_sem,
):
    row, c = lax.axis_index("row"), lax.axis_index("col")
    y, z = row // LINE, row % LINE
    place = {"y": y, "z": z, "c": c}

    def target(axis, t):
        if axis == "y":
            return (t * LINE + z, c)
        if axis == "z":
            return (y * LINE + t, c)
        return (row, t)

    def others(axis):
        return [(place[axis] + d) % LINE for d in range(1, LINE)]

    def copy(phase, axis, t, src, dst, mine):
        return pltpu.make_async_remote_copy(
            src_ref=src, dst_ref=dst, send_sem=send_sem.at[phase, t], recv_sem=recv_sem.at[phase, mine],
            device_id=target(axis, t), device_id_type=MESH,
        )

    started = []

    def push(phase, axis, src, dst):
        me = place[axis]
        for t in others(axis):
            op = copy(phase, axis, t, src(t), dst(me), me)
            op.start()
            started.append(op)

    def arrived(phase, axis, dst):
        for t in others(axis):
            copy(phase, axis, t, dst(t), dst(t), t).wait_recv()

    barrier = pltpu.get_barrier_semaphore()
    for axis in ("y", "z", "c"):
        for t in others(axis):
            pl.semaphore_signal(barrier, inc=1, device_id=target(axis, t), device_id_type=MESH)
    load = pltpu.make_async_copy(a_ref, raw, local_sem)
    load.start()

    indices = index_ref[...].astype(F32)
    for t in range(LINE):
        meta[t, :, :128] = sends_ref[:, t // 2 * 128 : t // 2 * 128 + 128]
        meta[t, :, 128:] = jnp.zeros((1, 128), I32)
        meta[t, :, 128 : 128 + R] = index_ref[...]
    couple = near_ref[...]
    to_lane = jnp.where(
        (iota((R, FAR * 128), 1) & 127) == iota((R, FAR * 128), 0) * FAR + (iota((R, FAR * 128), 1) >> 7), 1.0, 0.0
    ).astype(BF16)
    high = jnp.dot((couple >> 4).astype(F32).astype(BF16), to_lane, preferred_element_type=F32)
    low = jnp.dot((couple & 15).astype(F32).astype(BF16), to_lane, preferred_element_type=F32)
    want = jnp.zeros((1, 128), F32)
    for k in range(FAR):
        at = slice(k * 128, k * 128 + 128)
        want = want + high[k + 1 : k + 2, at] * 16.0 + low[k + 1 : k + 2, at]
    want = want.astype(I32)
    widen = jnp.where(iota((R, 512), 1) >> 5 == iota((R, 512), 0), 1.0, 0.0).astype(BF16)
    idx_all[c] = jnp.dot(
        jnp.broadcast_to(indices, (8, R)).astype(BF16), widen, preferred_element_type=F32
    )[:1]
    r = iota((512, 1), 0)
    order[...] = jnp.where(iota((512, 512), 1) == (r & 31) * R + (r >> 5), 1.0, 0.0).astype(BF16)
    for w in range(32):
        tall[w * R : w * R + R, K * 128 :] = p_ref[:, w * 128 : w * 128 + 128]
    own[...] = jnp.dot(order[...], tall[:, K * 128 :], preferred_element_type=F32).astype(BF16)
    panel[c] = own[...].astype(F32).T.astype(BF16)
    pl.semaphore_wait(barrier, 3 * (LINE - 1))

    def stripe(s):
        return pl.ds(pl.multiple_of(s * 256, 256), 256)

    def rows(start, count):
        return pl.ds(pl.multiple_of(start, count), count)

    push(META1, "y", lambda t: meta.at[t], lambda s: meta_y.at[s])
    push(SPREAD_Y, "y", lambda t: p_ref.at[:, stripe(t)], lambda s: store_y.at[rows(z * 128 + s * R, R)])
    push(SPREAD_Z, "z", lambda t: p_ref.at[:, stripe(LINE + t)], lambda s: store_z.at[rows(y * 128 + s * R, R)])
    push(PINDEX, "c", lambda t: idx_all.at[c], lambda s: idx_all.at[s])
    push(PANEL, "c", lambda t: panel.at[c], lambda s: panel.at[s])
    meta_y[y] = meta[y]
    store_y[rows(z * 128 + y * R, R)] = p_ref[:, stripe(y)]
    store_z[rows(y * 128 + z * R, R)] = p_ref[:, stripe(LINE + z)]
    arrived(META1, "y", lambda s: meta_y.at[s])
    push(META2, "z", lambda t: meta_y, lambda s: meta_all.at[s])

    def block(store, n):
        return store.at[rows(n % LINE * 128, 128)]

    def hand(phase, axis, store, n, t, follow):
        ref = block(store, n)
        op = pltpu.make_async_remote_copy(
            src_ref=ref, dst_ref=ref, send_sem=send_sem.at[follow, t % LINE], recv_sem=recv_sem.at[phase, n % LINE],
            device_id=target(axis, t % LINE), device_id_type=MESH,
        )
        op.start()
        started.append(op)

    def landed(phase, axis, store, n):
        copy(phase, axis, n % LINE, block(store, n), block(store, n), n % LINE).wait_recv()

    arrived(SPREAD_Y, "y", lambda s: store_y.at[rows(z * 128 + s * R, R)])
    for d in (2, 6, 1, 7):
        hand(FWD_Y, "z", store_y, z, z + d, FWD_Y)
    arrived(SPREAD_Z, "z", lambda s: store_z.at[rows(y * 128 + s * R, R)])
    for d in (2, 6, 1, 7):
        hand(FWD_Z, "y", store_z, y, y + d, FWD_Z)

    meta_all[z] = meta_y[...]
    arrived(META2, "z", lambda s: meta_all.at[s])
    for s in range(LINE):
        for t in range(LINE):
            table[pl.ds(t * LINE + s, 1), :] = meta_all[s, t]
    rows_of = table[:, :128].astype(F32)
    index_of = table[:, 128:].astype(F32)
    source = iota((64, 128), 0)
    lane = iota((64, 128), 1)
    remote = want - R
    total = jnp.zeros((64, 128), F32)
    for s in range(LINE):
        column = jnp.sum(jnp.where(lane == y % 2 * 64 + z * LINE + s, rows_of, 0.0), axis=1, keepdims=True)
        value = column + (source * R).astype(F32)
        total = total + jnp.where(source * LINE + s == remote, value, 0.0)
    fine = jnp.where(want < R, want + row * R, jnp.sum(total, axis=0, keepdims=True).astype(I32))
    request[...] = fine
    req_y[y] = fine
    req_z[z] = fine
    push(REQ_Y, "y", lambda t: request, lambda s: req_y.at[s])
    push(REQ_Z, "z", lambda t: request, lambda s: req_z.at[s])
    for d in (6, 2):
        for phase, follow, axis, store in ((FWD_Y, NEXT_Y, "z", store_y), (FWD_Z, NEXT_Z, "y", store_z)):
            me = place[axis]
            landed(phase, axis, store, me + d)
            if d == 6:
                hand(phase, axis, store, me + 6, me + 2, follow)
            hand(phase, axis, store, me + d, me + 8 - d // 2 if d == 2 else me + 1, follow)
    total = jnp.zeros((64, 128), F32)
    for t in range(R):
        total = total + jnp.where(source * R + t == fine, index_of[:, t : t + 1], 0.0)
    half_of = jnp.sum(total, axis=0, keepdims=True)

    def make_pick(n, _):
        r = iota((128, 1), 0)
        col = (r & 63)
        f = ((r >> 6) & 1) * 512 + (col & 1) * 256 + (col >> 2) * 16 + ((col >> 1) & 1) * 8 + n
        pick[rows(n * 128, 128), :] = jnp.where(iota((128, 1024), 1) == f, 1.0, 0.0).astype(BF16)
        return 0

    lax.fori_loop(0, 8, make_pick, 0)

    load.wait()
    for k in range(K):
        for w in range(32):
            tall[w * R : w * R + R, k * 128 : k * 128 + 128] = raw[k, :, w * 128 : w * 128 + 128]
    for k in range(K):
        at = slice(k * 128, k * 128 + 128)
        natural[:, at] = jnp.dot(order[...], tall[:, at], preferred_element_type=F32).astype(BF16)
    nothing = jnp.zeros((32, 128), BF16)
    for j in range(ASKED):
        b, slot = j // 8, j % 8
        i, k = j // FAR, 1 + j % FAR
        at = slice(slot * 128, slot * 128 + 128)
        here = b * 64 + (i - 8 * b // FAR) * 32
        there = 2 * b * 64 + 32 - here
        spread[here : here + 32, at] = natural[i * 32 : i * 32 + 32, k * 128 : k * 128 + 128]
        spread[there : there + 32, at] = nothing
    for n in range(4):
        terms[n] = jnp.dot(
            spread[...], pick[:, n * 256 : n * 256 + 256], preferred_element_type=F32
        ).astype(BF16)

    left = iota((128, 128), 1) < 64

    def join(out, count):
        both = []
        for pr in range(2):
            u0, u1 = (out[(2 * pr + n) * count : (2 * pr + n + 1) * count] for n in range(2))
            v0, v1 = (out[(4 + 2 * pr + n) * count : (5 + 2 * pr + n) * count] for n in range(2))
            both.append(jnp.where(left[:count], u0 + pltpu.roll(u1, 64, 1), pltpu.roll(v0, 64, 1) + v1))
        return both

    r = iota((512, 1), 0)
    f = ((r >> 6) & 1) * 256 + (r & 1) * 128 + (r >> 7) * 32 + ((r & 63) >> 1)
    own_pick[...] = jnp.where(iota((512, 512), 1) == f, 1.0, 0.0).astype(BF16)
    own_spread[...] = jnp.zeros_like(own_spread)
    for i in range(R):
        own_spread[i * 32 : i * 32 + 32, i % 4 * 128 : i % 4 * 128 + 128] = natural[i * 32 : i * 32 + 32, :128]
    own_terms[...] = jnp.dot(own_spread[...], own_pick[...], preferred_element_type=F32).astype(BF16)
    upper = idx_all[c]
    for q in range(4):
        at = slice(q * 128, q * 128 + 128)
        pieces = []
        for m in (1.0 - upper[:, at], upper[:, at]):
            for n in range(4):
                pieces.append(own_terms[at, n * 128 : n * 128 + 128] * m.astype(BF16))
        out = jnp.dot(jnp.concatenate(pieces, axis=0), own[at], preferred_element_type=F32)
        for pr, value in enumerate(join(out, 128)):
            ap[pr, at, :] = value

    eye = iota((128, 128), 0) == iota((128, 128), 1)

    def seek(req, hot, axis, swap):
        n = iota((1, 1024), 1)
        if swap:
            n = ((n >> 4) & 7) * 128 + (n >> 7) * R + (n & 15)

        def one(t, _):
            column = jnp.sum(jnp.where(eye, req[t], 0).astype(F32), axis=1, keepdims=True)[:ASKED].astype(I32)
            hot[t] = jnp.where(n == column, 1.0, 0.0).astype(BF16)
            return 0

        lax.fori_loop(0, LINE, one, 0)

    def serve(hot, t, store):
        got = jnp.dot(hot[t], store[...], preferred_element_type=F32).reshape(GROUPS, 8, 256)
        return jnp.concatenate([got[:, :, :128], got[:, :, 128:]], axis=1).astype(BF16)

    arrived(REQ_Y, "y", lambda s: req_y.at[s])
    arrived(REQ_Z, "z", lambda s: req_z.at[s])
    seek(req_y, hot_y, "y", True)
    seek(req_z, hot_z, "z", False)
    for d in (1, 7, 3, 5, 4):
        landed(FWD_Y, "z", store_y, z + d)
        landed(FWD_Z, "y", store_z, y + d)
    for d in (4, 3, 5, 2, 6, 1, 7):
        t = (y + d) % LINE
        pack_y[t] = serve(hot_y, t, store_y)
        op = copy(GHOST_Y, "y", t, pack_y.at[t], ghost.at[:, rows(y * 16, 16), :], y)
        op.start()
        started.append(op)
        t = (z + d) % LINE
        pack_z[t] = serve(hot_z, t, store_z)
        op = copy(GHOST_Z, "z", t, pack_z.at[t], ghost.at[:, rows(128 + z * 16, 16), :], z)
        op.start()
        started.append(op)
    ghost[:, rows(y * 16, 16), :] = serve(hot_y, y, store_y)
    ghost[:, rows(128 + z * 16, 16), :] = serve(hot_z, z, store_z)

    by_group = jnp.where(iota((16, 128), 1) >> 3 == iota((16, 128), 0), half_of, 0.0)
    by_slot = jnp.where((iota((128, 256), 0) & 7) == (iota((128, 256), 1) & 7), 1.0, 0.0)
    mask = jnp.dot(by_group.astype(BF16), by_slot.astype(BF16), preferred_element_type=F32)
    for b in range(GROUPS):
        upper = mask[b : b + 1]
        for h, m in ((0, 1.0 - upper), (1, upper)):
            for n in range(4):
                lhs[b, h * 256 + n * 64 : h * 256 + n * 64 + 64, :] = (
                    terms[n, b * 64 : b * 64 + 64, :] * m.astype(BF16)
                )
    arrived(PANEL, "c", lambda s: panel.at[s])
    arrived(PINDEX, "c", lambda s: idx_all.at[s])

    def make_wide(n, _):
        upper = idx_all[n]
        for h, m in ((0, 1.0 - upper), (1, upper)):
            for pr in range(2):
                wide[rows(n * 128 + h * 64, 64), pr * 512 : pr * 512 + 512] = (
                    panel[n, pr * 64 : pr * 64 + 64, :] * m.astype(BF16)
                )
        return 0

    lax.fori_loop(0, LINE, make_wide, 0)

    arrived(GHOST_Y, "y", lambda s: ghost.at[:, rows(s * 16, 16), :])
    arrived(GHOST_Z, "z", lambda s: ghost.at[:, rows(128 + s * 16, 16), :])

    for b in range(GROUPS):
        out = jnp.dot(lhs[b], ghost[b], preferred_element_type=F32)
        start = 8 * b // FAR * 32
        for pr, value in enumerate(join(out, 64)):
            ap[pr, start : start + 64, :] += value
    for pr in range(2):
        apb[pr * 512 : pr * 512 + 512] = ap[pr].astype(BF16)

    for n in range(LINE):
        value = jnp.dot(wide[n * 128 : n * 128 + 128, :], apb[...], preferred_element_type=F32)
        value = value.reshape(LINE, 2, 8, 128)
        partial[n] = value
        send_y[n] = value[:, 0].reshape(64, 128).astype(BF16)
    push(SUM_Y, "y", lambda t: send_y.at[t], lambda s: sum_y.at[s])
    for n in range(LINE):
        send_z[n] = partial[:, n, 1].reshape(64, 128).astype(BF16)
    push(SUM_Z, "z", lambda t: send_z.at[t], lambda s: sum_z.at[s])
    arrived(SUM_Y, "y", lambda s: sum_y.at[s])
    acc = partial[y, :, 0].reshape(64, 128)
    for t in others("y"):
        acc = acc + sum_y[t].astype(F32)
    half_y[...] = acc.reshape(LINE, 8, 128)
    push(LAST_Y, "z", lambda t: half_y.at[t], lambda s: last_y.at[s])
    arrived(SUM_Z, "z", lambda s: sum_z.at[s])
    acc = partial[:, z, 1].reshape(64, 128)
    for t in others("z"):
        acc = acc + sum_z[t].astype(F32)
    half_z[...] = acc.reshape(LINE, 8, 128)
    push(LAST_Z, "y", lambda t: half_z.at[t], lambda s: last_z.at[s])
    arrived(LAST_Y, "z", lambda s: last_y.at[s])
    acc = half_y[z]
    for t in others("z"):
        acc = acc + last_y[t]
    out_ref[0:8] = acc
    arrived(LAST_Z, "y", lambda s: last_z.at[s])
    acc = half_z[y]
    for t in others("y"):
        acc = acc + last_z[t]
    out_ref[8:16] = acc
    for op in started:
        op.wait_send()


def shards(a_tiles, neighbors, send_rows, p_tiles, p_index):
    vmem = pl.BlockSpec(memory_space=pltpu.VMEM)
    V = pltpu.VMEM
    return pl.pallas_call(
        kernel,
        out_shape=jax.ShapeDtypeStruct((R, 128), F32),
        in_specs=[vmem, pl.BlockSpec(memory_space=pl.ANY), vmem, vmem, vmem],
        out_specs=vmem,
        scratch_shapes=[
            V((K, R, 4096), BF16), V((LINE, 1, 256), I32),
            V((1024, 256), BF16), V((1024, 256), BF16),
            V((LINE, 1, 256), I32), V((LINE, LINE, 1, 256), I32), V((64, 256), I32),
            V((1, 128), I32), V((LINE, 1, 128), I32), V((LINE, 1, 128), I32),
            V((LINE, ASKED, 1024), BF16), V((LINE, ASKED, 1024), BF16),
            V((LINE, GROUPS, 16, 128), BF16), V((LINE, GROUPS, 16, 128), BF16),
            V((GROUPS, 256, 128), BF16),
            V((LINE, 128, 512), BF16), V((LINE, 1, 512), F32),
            V((512, 512), BF16), V((512, 1024), BF16), V((512, K * 128), BF16), V((512, 128), BF16),
            V((1024, 1024), BF16), V((GROUPS * 64, 1024), BF16), V((4, GROUPS * 64, 256), BF16),
            V((GROUPS, 512, 256), BF16), V((1024, 1024), BF16),
            V((512, 512), BF16), V((512, 512), BF16), V((512, 512), BF16),
            V((2, 512, 128), F32), V((1024, 128), BF16), V((LINE, LINE, 2, 8, 128), F32),
            V((LINE, 64, 128), BF16), V((LINE, 64, 128), BF16),
            V((LINE, 64, 128), BF16), V((LINE, 64, 128), BF16),
            V((LINE, 8, 128), F32), V((LINE, 8, 128), F32),
            V((LINE, 8, 128), F32), V((LINE, 8, 128), F32),
            pltpu.SemaphoreType.DMA((18, LINE)), pltpu.SemaphoreType.DMA((16, LINE)), pltpu.SemaphoreType.DMA,
        ],
        compiler_params=pltpu.CompilerParams(
            collective_id=0, has_side_effects=True, vmem_limit_bytes=48 * 2**20
        ),
    )(
        p_tiles.reshape(R, 4096),
        a_tiles.transpose(1, 0, 2),
        neighbors.T,
        send_rows,
        p_index.reshape(1, R),
    )


def solution(mesh):
    in_specs = (
        P("row", None, None),
        P("row", None),
        P("row", None),
        P("row", "col", None),
        P("row", "col"),
    )
    return jax.shard_map(shards, mesh=mesh, in_specs=in_specs, out_specs=P("row", "col"), check_vma=False)
```

time: 72.7 us -> 59.6 us (0.82)
  Pallas kernels: 65.3 us -> 55.3 us
  local copies, waits for them, and re-layouts: 5.48 us -> 3.38 us
    pallas_call x1, Pallas kernels: 65.3 us -> 55.3 us  [shards(): pl.pallas_call(kernel, out_shape=jax.ShapeDtypeStruct((R, 128), F32), in_...]
    another operation x1 -> x0, local copies, waits for them, and re-layouts: 0.97 us -> none  [shards(): tall = tiles.reshape(R * 32, 128)]
    unnamed x12 -> x11, local copies, waits for them, and re-layouts: 4.03 us -> 3.38 us
where the time goes in v2:
time: 59.6 us; the launch traced here: 58.7 us
  Pallas kernels  55.3 us (93%)
  local copies, waits for them, and re-layouts  3.38 us (6%)
    pallas_call x1, Pallas kernels, shards(): pl.pallas_call(kernel, out_shape=jax.ShapeDtypeStruct((R, 128), F32), in_...  55.3 us
    unnamed x11, local copies, waits for them, and re-layouts  3.38 us

profile of v2, /device:TPU:1, one launch (start us, length us, event | category | flops | bytes accessed | tf_op | source)
XLA Modules:
  0.0 58.7 jit_solution(13778328501937344601)
XLA Ops:
  0.0 0.0 copy-start.2
  0.0 0.0 copy-start.3
  0.0 0.0 copy-start.4
  0.0 0.7 %copy-done.2 = s32[16,7]{0,1:T(8,128)S(1)} copy-done((s32[16,7]{0,1:T(8,128)S(1)}, s32[16,7]{0,1:T(8,128)}, u32[]{:S(2)}) %copy-start.2) | copy-done | bytes 472
  0.7 0.0 copy-done.3
  0.7 0.0 copy-done.4
  0.7 0.0 copy-start
  0.7 1.2 %copy-done = bf16[16,7,4096]{2,0,1:T(8,128)(2,1)S(1)} copy-done((bf16[16,7,4096]{2,0,1:T(8,128)(2,1)S(1)}, bf16[16,7,4096]{2,0,1:T(8,128)(2,1)}, u32[]{:S(2)}) %copy-start) | copy-done | bytes 917528
  1.9 0.0 copy-start.1
  1.9 0.9 %copy-done.1 = bf16[16,1,4096]{2,0,1:T(8,128)(2,1)S(1)} copy-done((bf16[16,1,4096]{2,0,1:T(8,128)(2,1)S(1)}, bf16[16,1,4096]{2,0,1:T(8,128)(2,1)}, u32[]{:S(2)}) %copy-start.1) | copy-done | bytes 131096
  2.8 55.3 %shard_map.55 = f32[16,128]{1,0:T(8,128)S(1)} custom-call(bf16[16,4096]{1,0:T(8,128)(2,1)S(1)} %bitcast.5, bf16[7,16,4096]{2,1,0:T(8,128)(2,1)S(1)} %bitcast.4, s32[7,16]{1,0:T(8,128)S(1)} %bitcast.6, s32[1,512]{1,0:T(1,128)S(1)} %copy-done.3, s32[1,16]{1,0:T(1,128)S(1)} %bitcast.7), custom_call_target="tpu_custom_call" | custom-call | tf_op jit(solution)/shard_map/pallas_call | solution.py:343
  58.1 0.6 %copy.7 = f32[16,128]{1,0:T(8,128)} copy(f32[16,128]{1,0:T(8,128)S(1)} %shard_map.55) | data formatting | bytes 16384
Async XLA Ops:
  0.0 0.7 %copy-start.2 = (s32[16,7]{0,1:T(8,128)S(1)}, s32[16,7]{0,1:T(8,128)}, u32[]{:S(2)}) copy-start(s32[16,7]{0,1:T(8,128)} %param.6) | copy-start | bytes 1348
  0.0 0.7 %copy-start.3 = (s32[1,512]{1,0:T(1,128)S(1)}, s32[1,512]{1,0:T(1,128)}, u32[]{:S(2)}) copy-start(s32[1,512]{1,0:T(1,128)} %sends_ref.1) | copy-start | bytes 6148
  0.0 0.7 %copy-start.4 = (s32[16,1]{0,1:T(1,128)S(1)}, s32[16,1]{0,1:T(1,128)}, u32[]{:S(2)}) copy-start(s32[16,1]{0,1:T(1,128)} %param.9) | copy-start | bytes 196
  0.7 1.2 %copy-start = (bf16[16,7,4096]{2,0,1:T(8,128)(2,1)S(1)}, bf16[16,7,4096]{2,0,1:T(8,128)(2,1)}, u32[]{:S(2)}) copy-start(bf16[16,7,4096]{2,0,1:T(8,128)(2,1)} %param.5) | copy-start | bytes 2752516
  1.9 0.9 %copy-start.1 = (bf16[16,1,4096]{2,0,1:T(8,128)(2,1)S(1)}, bf16[16,1,4096]{2,0,1:T(8,128)(2,1)}, u32[]{:S(2)}) copy-start(bf16[16,1,4096]{2,0,1:T(8,128)(2,1)} %param.8) | copy-start | bytes 393220

commit v3 on v2

--- a/solution.py
+++ b/solution.py
@@ -15,7 +15,7 @@
 ASKED = R * FAR
 GROUPS = ASKED // 8
 F32, BF16, I32 = jnp.float32, jnp.bfloat16, jnp.int32
-META1, SPREAD_Y, SPREAD_Z, PANEL, PINDEX, META2, FWD_Y, FWD_Z, REQ_Y, REQ_Z, GHOST_Y, GHOST_Z, SUM_Y, SUM_Z, LAST_Y, LAST_Z, NEXT_Y, NEXT_Z = range(18)
+META1, SPREAD_Y, SPREAD_Z, PANEL, PINDEX, META2, REQ_Y, REQ_Z, GHOST_Y, GHOST_Z, SUM_Y, SUM_Z, LAST_Y, LAST_Z = range(14)
 
 
 def iota(shape, dim):
@@ -23,12 +23,13 @@
 
 
 def kernel(
-    p_ref, a_ref, near_ref, sends_ref, index_ref, out_ref,
-    raw, meta, store_y, store_z, meta_y, meta_all, table, request, req_y, req_z, hot_y, hot_z,
+    p_ref, a_ref, near_in, sends_in, index_in, out_ref,
+    near_ref, sends_ref, index_ref,
+    raw, mine, meta, store_y, store_z, meta_y, meta_all, table, request, req_y, req_z, hot_y, hot_z,
     pack_y, pack_z, ghost, panel, idx_all, order, tall, natural, own, pick, spread, terms, lhs, wide,
     own_pick, own_spread, own_terms,
     ap, apb, partial, send_y, send_z, sum_y, sum_z, half_y, half_z, last_y, last_z,
-    send_sem, recv_sem, local_sem,
+    send_sem, recv_sem, leg_sem, part_sem, next_sem, far_sem, block_sem, local_sem,
 ):
     row, c = lax.axis_index("row"), lax.axis_index("col")
     y, z = row // LINE, row % LINE
@@ -67,14 +68,97 @@
     for axis in ("y", "z", "c"):
         for t in others(axis):
             pl.semaphore_signal(barrier, inc=1, device_id=target(axis, t), device_id_type=MESH)
-    load = pltpu.make_async_copy(a_ref, raw, local_sem)
-    load.start()
-
-    indices = index_ref[...].astype(F32)
+    load = pltpu.make_async_copy(a_ref, raw, local_sem.at[0])
+    fetch = pltpu.make_async_copy(p_ref, mine, local_sem.at[1])
+    small = [
+        pltpu.make_async_copy(src, dst, local_sem.at[2 + n])
+        for n, (src, dst) in enumerate(((sends_in, sends_ref), (index_in, index_ref), (near_in, near_ref)))
+    ]
+    for op in small + [fetch, load]:
+        op.start()
+    small[0].wait()
+    small[1].wait()
+
     for t in range(LINE):
         meta[t, :, :128] = sends_ref[:, t // 2 * 128 : t // 2 * 128 + 128]
         meta[t, :, 128:] = jnp.zeros((1, 128), I32)
         meta[t, :, 128 : 128 + R] = index_ref[...]
+    pl.semaphore_wait(barrier, 3 * (LINE - 1))
+
+    def stripe(s):
+        return pl.ds(pl.multiple_of(s * 256, 256), 256)
+
+    def rows(start, count):
+        return pl.ds(pl.multiple_of(start, count), count)
+
+    push(META1, "y", lambda t: meta.at[t], lambda s: meta_y.at[s])
+    push(SPREAD_Y, "y", lambda t: p_ref.at[:, stripe(t)], lambda s: store_y.at[rows(z * 128 + s * R, R)])
+    push(SPREAD_Z, "z", lambda t: p_ref.at[:, stripe(LINE + t)], lambda s: store_z.at[rows(y * 128 + s * R, R)])
+    meta_y[y] = meta[y]
+    fetch.wait()
+    store_y[rows(z * 128 + y * R, R)] = mine[:, stripe(y)]
+    store_z[rows(y * 128 + z * R, R)] = mine[:, stripe(LINE + z)]
+    arrived(META1, "y", lambda s: meta_y.at[s])
+    push(META2, "z", lambda t: meta_y, lambda s: meta_all.at[s])
+
+    roles = ((store_y, "z", z), (store_z, "y", y))
+
+    def part(role, n, h):
+        return roles[role][0].at[rows(n % LINE * 128 + h * 64, 64)]
+
+    def block(role, n):
+        return roles[role][0].at[rows(n % LINE * 128, 128)]
+
+    def hand(role, ref, leg, step, recv):
+        _, axis, me = roles[role]
+        op = pltpu.make_async_remote_copy(
+            src_ref=ref, dst_ref=ref, send_sem=leg_sem.at[role, leg], recv_sem=recv,
+            device_id=target(axis, (me + step) % LINE), device_id_type=MESH,
+        )
+        op.start()
+        started.append(op)
+
+    def await_ref(role, ref, recv):
+        _, axis, me = roles[role]
+        pltpu.make_async_remote_copy(
+            src_ref=ref, dst_ref=ref, send_sem=leg_sem.at[role, 0], recv_sem=recv,
+            device_id=target(axis, (me + 1) % LINE), device_id_type=MESH,
+        ).wait_recv()
+
+    def first(role):
+        me = roles[role][2]
+        hand(role, part(role, me, 0), 0, 2, part_sem.at[role, 0, 0])
+        hand(role, part(role, me, 1), 1, 6, part_sem.at[role, 1, 1])
+        hand(role, part(role, me, 1), 2, 2, part_sem.at[role, 0, 1])
+        hand(role, part(role, me, 0), 3, 6, part_sem.at[role, 1, 0])
+        hand(role, block(role, me), 4, 1, block_sem.at[role, me])
+        hand(role, block(role, me), 5, 7, block_sem.at[role, me])
+
+    def second(role, back, h):
+        me = roles[role][2]
+        n, onward, far = (me + 6, 1, 2) if back == 0 else (me + 2, 7, 6)
+        ref = part(role, n, h)
+        await_ref(role, ref, part_sem.at[role, back, h])
+        if h == back:
+            hand(role, ref, 6 + back, far, far_sem.at[role, h])
+        hand(role, ref, 8 + 2 * back + h, onward, next_sem.at[role, back, h])
+
+    def landed(role):
+        me = roles[role][2]
+        for d in (1, 7):
+            await_ref(role, block(role, me + d), block_sem.at[role, (me + d) % LINE])
+        for h in range(2):
+            await_ref(role, part(role, me + 5, h), next_sem.at[role, 0, h])
+            await_ref(role, part(role, me + 3, h), next_sem.at[role, 1, h])
+            await_ref(role, part(role, me + 4, h), far_sem.at[role, h])
+
+    arrived(SPREAD_Y, "y", lambda s: store_y.at[rows(z * 128 + s * R, R)])
+    first(0)
+    arrived(SPREAD_Z, "z", lambda s: store_z.at[rows(y * 128 + s * R, R)])
+    first(1)
+
+    indices = index_ref[...].astype(F32)
+    small[2].wait()
     couple = near_ref[...]
     to_lane = jnp.where(
         (iota((R, FAR * 128), 1) & 127) == iota((R, FAR * 128), 0) * FAR + (iota((R, FAR * 128), 1) >> 7), 1.0, 0.0
@@ -93,49 +177,24 @@
     r = iota((512, 1), 0)
     order[...] = jnp.where(iota((512, 512), 1) == (r & 31) * R + (r >> 5), 1.0, 0.0).astype(BF16)
     for w in range(32):
-        tall[w * R : w * R + R, K * 128 :] = p_ref[:, w * 128 : w * 128 + 128]
+        tall[w * R : w * R + R, K * 128 :] = mine[:, w * 128 : w * 128 + 128]
     own[...] = jnp.dot(order[...], tall[:, K * 128 :], preferred_element_type=F32).astype(BF16)
     panel[c] = own[...].astype(F32).T.astype(BF16)
-    pl.semaphore_wait(barrier, 3 * (LINE - 1))
-
-    def stripe(s):
-        return pl.ds(pl.multiple_of(s * 256, 256), 256)
-
-    def rows(start, count):
-        return pl.ds(pl.multiple_of(start, count), count)
-
-    push(META1, "y", lambda t: meta.at[t], lambda s: meta_y.at[s])
-    push(SPREAD_Y, "y", lambda t: p_ref.at[:, stripe(t)], lambda s: store_y.at[rows(z * 128 + s * R, R)])
-    push(SPREAD_Z, "z", lambda t: p_ref.at[:, stripe(LINE + t)], lambda s: store_z.at[rows(y * 128 + s * R, R)])
     push(PINDEX, "c", lambda t: idx_all.at[c], lambda s: idx_all.at[s])
     push(PANEL, "c", lambda t: panel.at[c], lambda s: panel.at[s])
-    meta_y[y] = meta[y]
-    store_y[rows(z * 128 + y * R, R)] = p_ref[:, stripe(y)]
-    store_z[rows(y * 128 + z * R, R)] = p_ref[:, stripe(LINE + z)]
-    arrived(META1, "y", lambda s: meta_y.at[s])
-    push(META2, "z", lambda t: meta_y, lambda s: meta_all.at[s])
-
-    def block(store, n):
-        return store.at[rows(n % LINE * 128, 128)]
-
-    def hand(phase, axis, store, n, t, follow):
-        ref = block(store, n)
-        op = pltpu.make_async_remote_copy(
-            src_ref=ref, dst_ref=ref, send_sem=send_sem.at[follow, t % LINE], recv_sem=recv_sem.at[phase, n % LINE],
-            device_id=target(axis, t % LINE), device_id_type=MESH,
-        )
-        op.start()
-        started.append(op)
-
-    def landed(phase, axis, store, n):
-        copy(phase, axis, n % LINE, block(store, n), block(store, n), n % LINE).wait_recv()
-
-    arrived(SPREAD_Y, "y", lambda s: store_y.at[rows(z * 128 + s * R, R)])
-    for d in (2, 6, 1, 7):
-        hand(FWD_Y, "z", store_y, z, z + d, FWD_Y)
-    arrived(SPREAD_Z, "z", lambda s: store_z.at[rows(y * 128 + s * R, R)])
-    for d in (2, 6, 1, 7):
-        hand(FWD_Z, "y", store_z, y, y + d, FWD_Z)
+
+    def make_pick(n, _):
+        r = iota((128, 1), 0)
+        col = (r & 63)
+        f = ((r >> 6) & 1) * 512 + (col & 1) * 256 + (col >> 2) * 16 + ((col >> 1) & 1) * 8 + n
+        pick[rows(n * 128, 128), :] = jnp.where(iota((128, 1024), 1) == f, 1.0, 0.0).astype(BF16)
+        return 0
+
+    lax.fori_loop(0, 8, make_pick, 0)
+
+    r = iota((512, 1), 0)
+    f = ((r >> 6) & 1) * 256 + (r & 1) * 128 + (r >> 7) * 32 + ((r & 63) >> 1)
+    own_pick[...] = jnp.where(iota((512, 512), 1) == f, 1.0, 0.0).astype(BF16)
 
     meta_all[z] = meta_y[...]
     arrived(META2, "z", lambda s: meta_all.at[s])
@@ -158,26 +217,13 @@
     req_z[z] = fine
     push(REQ_Y, "y", lambda t: request, lambda s: req_y.at[s])
     push(REQ_Z, "z", lambda t: request, lambda s: req_z.at[s])
-    for d in (6, 2):
-        for phase, follow, axis, store in ((FWD_Y, NEXT_Y, "z", store_y), (FWD_Z, NEXT_Z, "y", store_z)):
-            me = place[axis]
-            landed(phase, axis, store, me + d)
-            if d == 6:
-                hand(phase, axis, store, me + 6, me + 2, follow)
-            hand(phase, axis, store, me + d, me + 8 - d // 2 if d == 2 else me + 1, follow)
+    for back, h in ((0, 0), (1, 1), (0, 1), (1, 0)):
+        for role in range(2):
+            second(role, back, h)
     total = jnp.zeros((64, 128), F32)
     for t in range(R):
         total = total + jnp.where(source * R + t == fine, index_of[:, t : t + 1], 0.0)
     half_of = jnp.sum(total, axis=0, keepdims=True)
-
-    def make_pick(n, _):
-        r = iota((128, 1), 0)
-        col = (r & 63)
-        f = ((r >> 6) & 1) * 512 + (col & 1) * 256 + (col >> 2) * 16 + ((col >> 1) & 1) * 8 + n
-        pick[rows(n * 128, 128), :] = jnp.where(iota((128, 1024), 1) == f, 1.0, 0.0).astype(BF16)
-        return 0
-
-    lax.fori_loop(0, 8, make_pick, 0)
 
     load.wait()
     for k in range(K):
@@ -210,9 +256,6 @@
             both.append(jnp.where(left[:count], u0 + pltpu.roll(u1, 64, 1), pltpu.roll(v0, 64, 1) + v1))
         return both
 
-    r = iota((512, 1), 0)
-    f = ((r >> 6) & 1) * 256 + (r & 1) * 128 + (r >> 7) * 32 + ((r & 63) >> 1)
-    own_pick[...] = jnp.where(iota((512, 512), 1) == f, 1.0, 0.0).astype(BF16)
     own_spread[...] = jnp.zeros_like(own_spread)
     for i in range(R):
         own_spread[i * 32 : i * 32 + 32, i % 4 * 128 : i % 4 * 128 + 128] = natural[i * 32 : i * 32 + 32, :128]
@@ -250,9 +293,8 @@
     arrived(REQ_Z, "z", lambda s: req_z.at[s])
     seek(req_y, hot_y, "y", True)
     seek(req_z, hot_z, "z", False)
-    for d in (1, 7, 3, 5, 4):
-        landed(FWD_Y, "z", store_y, z + d)
-        landed(FWD_Z, "y", store_z, y + d)
+    for role in range(2):
+        landed(role)
     for d in (4, 3, 5, 2, 6, 1, 7):
         t = (y + d) % LINE
         pack_y[t] = serve(hot_y, t, store_y)
@@ -343,10 +385,11 @@
     return pl.pallas_call(
         kernel,
         out_shape=jax.ShapeDtypeStruct((R, 128), F32),
-        in_specs=[vmem, pl.BlockSpec(memory_space=pl.ANY), vmem, vmem, vmem],
+        in_specs=[pl.BlockSpec(memory_space=pl.ANY)] * 5,
         out_specs=vmem,
         scratch_shapes=[
-            V((K, R, 4096), BF16), V((LINE, 1, 256), I32),
+            V((K, R), I32), V((1, LINE * 64), I32), V((1, R), I32),
+            V((K, R, 4096), BF16), V((R, 4096), BF16), V((LINE, 1, 256), I32),
             V((1024, 256), BF16), V((1024, 256), BF16),
             V((LINE, 1, 256), I32), V((LINE, LINE, 1, 256), I32), V((64, 256), I32),
             V((1, 128), I32), V((LINE, 1, 128), I32), V((LINE, 1, 128), I32),
@@ -363,10 +406,12 @@
             V((LINE, 64, 128), BF16), V((LINE, 64, 128), BF16),
             V((LINE, 8, 128), F32), V((LINE, 8, 128), F32),
             V((LINE, 8, 128), F32), V((LINE, 8, 128), F32),
-            pltpu.SemaphoreType.DMA((18, LINE)), pltpu.SemaphoreType.DMA((16, LINE)), pltpu.SemaphoreType.DMA,
+            pltpu.SemaphoreType.DMA((14, LINE)), pltpu.SemaphoreType.DMA((14, LINE)),
+            pltpu.SemaphoreType.DMA((2, 12)), pltpu.SemaphoreType.DMA((2, 2, 2)), pltpu.SemaphoreType.DMA((2, 2, 2)),
+            pltpu.SemaphoreType.DMA((2, 2)), pltpu.SemaphoreType.DMA((2, LINE)), pltpu.SemaphoreType.DMA((5,)),
         ],
         compiler_params=pltpu.CompilerParams(
-            collective_id=0, has_side_effects=True, vmem_limit_bytes=48 * 2**20
+            collective_id=0, has_side_effects=True, vmem_limit_bytes=56 * 2**20
         ),
     )(
         p_tiles.reshape(R, 4096),

time: 59.6 us -> 58.5 us (0.982); the launches traced: 58.7 us -> 58.4 us
  local copies, waits for them, and re-layouts: 3.38 us -> 1.3 us
  Pallas kernels: 55.3 us -> 57.1 us
    unnamed x11 -> x1, local copies, waits for them, and re-layouts: 3.38 us -> 1.3 us
    pallas_call x1, Pallas kernels: 55.3 us -> 57.1 us  [shards(): pl.pallas_call(kernel, out_shape=jax.ShapeDtypeStruct((R, 128), F32), in_...]
where the time goes in v3:
time: 58.5 us; the launch traced here: 58.4 us
  Pallas kernels  57.1 us (98%)
  local copies, waits for them, and re-layouts  1.3 us (2%)
    pallas_call x1, Pallas kernels, shards(): pl.pallas_call(kernel, out_shape=jax.ShapeDtypeStruct((R, 128), F32), in_...  57.1 us
    unnamed x1, local copies, waits for them, and re-layouts  1.3 us

profile of v3, /device:TPU:1, one launch (start us, length us, event | category | flops | bytes accessed | tf_op | source)
XLA Modules:
  0.0 58.4 jit_solution(16194772865074060584)
XLA Ops:
  0.0 57.1 %shard_map.55 = f32[16,128]{1,0:T(8,128)} custom-call(bf16[16,4096]{1,0:T(8,128)(2,1)} %bitcast.5, bf16[7,16,4096]{2,1,0:T(8,128)(2,1)} %bitcast.4, s32[7,16]{1,0:T(8,128)} %bitcast.6, s32[1,512]{1,0:T(1,128)} %sends_in.1, s32[1,16]{1,0:T(1,128)} %bitcast.7), custom_call_target="tpu_custom_call" | custom-call | tf_op jit(solution)/shard_map/pallas_call | solution.py:385
  57.1 1.3 %copy.7 = f32[16,128]{1,0:T(8,128)} copy(f32[16,128]{1,0:T(8,128)} %shard_map.55) | data formatting | bytes 16384

commit v4 on v3

--- a/solution.py
+++ b/solution.py
@@ -91,9 +91,9 @@
     def rows(start, count):
         return pl.ds(pl.multiple_of(start, count), count)
 
-    push(META1, "y", lambda t: meta.at[t], lambda s: meta_y.at[s])
     push(SPREAD_Y, "y", lambda t: p_ref.at[:, stripe(t)], lambda s: store_y.at[rows(z * 128 + s * R, R)])
     push(SPREAD_Z, "z", lambda t: p_ref.at[:, stripe(LINE + t)], lambda s: store_z.at[rows(y * 128 + s * R, R)])
+    push(META1, "y", lambda t: meta.at[t], lambda s: meta_y.at[s])
     meta_y[y] = meta[y]
     fetch.wait()
     store_y[rows(z * 128 + y * R, R)] = mine[:, stripe(y)]
@@ -344,11 +344,9 @@
     for pr in range(2):
         apb[pr * 512 : pr * 512 + 512] = ap[pr].astype(BF16)
 
+    partial[...] = jnp.dot(wide[...], apb[...], preferred_element_type=F32).reshape(LINE, LINE, 2, 8, 128)
     for n in range(LINE):
-        value = jnp.dot(wide[n * 128 : n * 128 + 128, :], apb[...], preferred_element_type=F32)
-        value = value.reshape(LINE, 2, 8, 128)
-        partial[n] = value
-        send_y[n] = value[:, 0].reshape(64, 128).astype(BF16)
+        send_y[n] = partial[n, :, 0].reshape(64, 128).astype(BF16)
     push(SUM_Y, "y", lambda t: send_y.at[t], lambda s: sum_y.at[s])
     for n in range(LINE):
         send_z[n] = partial[:, n, 1].reshape(64, 128).astype(BF16)

time: 58.5 us -> 58.7 us (level)
  no operation moved by 1% of the time
where the time goes in v4:
time: 58.7 us; the launch traced here: 58.5 us
  Pallas kernels  57.2 us (97%)
  local copies, waits for them, and re-layouts  1.3 us (2%)
    pallas_call x1, Pallas kernels, shards(): pl.pallas_call(kernel, out_shape=jax.ShapeDtypeStruct((R, 128), F32), in_...  57.2 us
    unnamed x1, local copies, waits for them, and re-layouts  1.3 us

profile of v4, /device:TPU:1, one launch (start us, length us, event | category | flops | bytes accessed | tf_op | source)
XLA Modules:
  0.0 58.5 jit_solution(18305050320325101313)
XLA Ops:
  0.0 57.2 %shard_map.55 = f32[16,128]{1,0:T(8,128)} custom-call(bf16[16,4096]{1,0:T(8,128)(2,1)} %bitcast.5, bf16[7,16,4096]{2,1,0:T(8,128)(2,1)} %bitcast.4, s32[7,16]{1,0:T(8,128)} %bitcast.6, s32[1,512]{1,0:T(1,128)} %sends_in.1, s32[1,16]{1,0:T(1,128)} %bitcast.7), custom_call_target="tpu_custom_call" | custom-call | tf_op jit(solution)/shard_map/pallas_call | solution.py:383
  57.2 1.3 %copy.7 = f32[16,128]{1,0:T(8,128)} copy(f32[16,128]{1,0:T(8,128)} %shard_map.55) | data formatting | bytes 16384
